TPU v7x, 512 devices: a whole 4x4x16 slice. The times are simulated.
512 devices in a mesh: seq: 32 (over x, y, core), key: 16 (over z).
Axes of the slice: x: 4, y: 4, z: 16, core: 2. Of those that a mesh axis runs over, the one named last changes fastest.
Arguments:
- query_rows: bfloat16 [8192, 16, 256], P('seq', None, 'key'), may hold values from -0.375 to 0.375
- key_rows: bfloat16 [8192, 16, 256], P('seq', None, 'key'), may hold values from -0.1875 to 0.1875
- value_rows: bfloat16 [8192, 16, 256], P('seq', 'key'), may hold values from -6 to 6
- out_grad: bfloat16 [8192, 16, 256], P('seq', 'key')
- log_gates: float32 [16, 8192], P('key', 'seq'), may hold values from -0.8 to 0, as said below
- write_rate: float32 [16, 8192], P('key', 'seq'), may hold values from 0.1 to 0.8
- group_inverse: bfloat16 [64, 16, 128, 128], P('seq', 'key'), as said below
- states: bfloat16 [64, 16, 256, 256], P('seq', None, 'key'), may hold values from -0.75 to 0.75
Outputs:
- grad_query: bfloat16 [8192, 16, 256], P('seq', None, 'key')
- grad_key: bfloat16 [8192, 16, 256], P('seq', None, 'key')
- grad_value: bfloat16 [8192, 16, 256], P('seq', 'key')
- grad_square: float32 [], replicated
Inputs may be any that keep to these rules, and one draw needn't show every extreme that they name: `group_inverse`: each group's matrix is unit lower triangular: ones on the diagonal, zeros above it. `log_gates`: every entry is the logarithm of a decay factor, never positive.
All inputs are finite; a program needn't handle non-finite values.
Results may differ from a plain program's by a relative error of at most 0.007.
Values may be sent and summed in bfloat16 or wider, within the bound.
No kernel may reach another device: no remote copies, remote signals or barrier semaphores. Data moves between devices by JAX's collectives and lax.ppermute only.
A program may use at most 128 MiB of HBM per device.

v0:
```python
import jax
import jax.numpy as jnp
from jax import lax
from jax.sharding import PartitionSpec as P

highest_mode = lax.Precision.HIGHEST


def from_behind(value, axis, steps):
    count = lax.axis_size(axis)
    first, last = (max(0, -steps), min(count, count - steps))
    return lax.ppermute(value, axis, [(source, source + steps) for source in range(first, last)])


def mixed_dot(form, left, right):
    return jnp.einsum(form, left, right, preferred_element_type=jnp.float32)


def precise_product(form, left, right):
    return jnp.einsum(form, left.astype(jnp.float32), right, precision=highest_mode)


def linear_part(state_in, write_block, key_block, decay_block):
    through = precise_product("thk,hkm->thm", key_block, state_in)
    return decay_block[:, None, None] * state_in - precise_product(
        "thk,thm->hkm", write_block, through
    )


def device_map(state_out, written_keys, key_result, end_decay, offset_term):

    def group_step(state_in, pieces):
        write_block, key_block, decay_block, offset_block = pieces
        return (linear_part(state_in, write_block, key_block, decay_block) + offset_block, state_in)

    return lax.scan(
        group_step, state_out, (written_keys, key_result, end_decay, offset_term), reverse=True
    )


def token_wise(factor):
    return jnp.transpose(factor, (0, 2, 1))[:, :, :, None]


def square_sum(array):
    return jnp.sum(jnp.square(array.astype(jnp.float32)))


def local(query_rows, key_rows, value_rows, out_grad, log_gates, write_rate, group_inverse, states):
    halfway_point = jnp.bfloat16
    query_heads, key_heads, state_heads = (
        lax.all_to_all(query_rows, "key", split_axis=1, concat_axis=2, tiled=True),
        lax.all_to_all(key_rows, "key", split_axis=1, concat_axis=2, tiled=True),
        lax.all_to_all(states, "key", split_axis=1, concat_axis=2, tiled=True),
    )
    group_count, head_local, group_len, _ = group_inverse.shape
    token_count, _, key_width = query_heads.shape
    value_width = value_rows.shape[2]
    query_blk = query_heads.reshape(group_count, group_len, head_local, key_width)
    key_blk = key_heads.reshape(group_count, group_len, head_local, key_width)
    value_blk = value_rows.reshape(group_count, group_len, head_local, value_width)
    grad_blk = out_grad.reshape(group_count, group_len, head_local, value_width)
    gate_blk = jnp.transpose(log_gates.reshape(head_local, group_count, group_len), (1, 0, 2))
    rate_blk = jnp.transpose(write_rate.reshape(head_local, group_count, group_len), (1, 0, 2))
    gamma = jnp.cumsum(gate_blk, axis=2)
    final_gamma_value = gamma[:, :, -1:]
    incoming_decay = jnp.exp(gamma)
    outgoing_decay = jnp.exp(final_gamma_value - gamma)
    row_ids = lax.broadcasted_iota(jnp.int32, (group_len, group_len), 0)
    col_ids = lax.broadcasted_iota(jnp.int32, (group_len, group_len), 1)
    lower = row_ids >= col_ids
    spread = gamma[:, :, :, None] - gamma[:, :, None, :]
    decay_mask = jnp.where(lower, jnp.exp(jnp.where(lower, spread, 0.0)), 0.0)
    key_scaled = (key_blk * token_wise(rate_blk * incoming_decay)).astype(halfway_point)
    written_keys = mixed_dot("nhts,nshk->nthk", group_inverse, key_scaled).astype(halfway_point)
    scaled_values = (value_blk * token_wise(rate_blk)).astype(halfway_point)
    fresh_values = (
        mixed_dot("nhts,nshv->nthv", group_inverse, scaled_values)
        - mixed_dot("nthk,nhkv->nthv", written_keys, state_heads)
    ).astype(halfway_point)
    score_mat = (mixed_dot("nthk,nshk->nhts", query_blk, key_blk) * decay_mask).astype(
        halfway_point
    )
    key_result = (key_blk * token_wise(outgoing_decay)).astype(halfway_point)
    incoming_query = (query_blk * token_wise(incoming_decay)).astype(halfway_point)
    inner_gradient = mixed_dot("nhts,nthv->nshv", score_mat, grad_blk)
    offset_term = mixed_dot("nthk,nthv->nhkv", incoming_query, grad_blk) - precise_product(
        "nthk,nthv->nhkv", written_keys, inner_gradient
    )
    end_decay = jnp.exp(final_gamma_value[:, :, 0])
    empty_state = jnp.zeros((head_local, key_width, value_width), jnp.float32)

    def relay_hop(hop_index, incoming):
        state_in, _ = device_map(incoming, written_keys, key_result, end_decay, offset_term)
        return from_behind(state_in, "seq", -1)

    state_out = lax.fori_loop(0, lax.axis_size("seq") - 1, relay_hop, empty_state)
    _, state_gradient = device_map(state_out, written_keys, key_result, end_decay, offset_term)
    value_rounding = (
        inner_gradient + precise_product("nthk,nhkv->nthv", key_result, state_gradient)
    ).astype(halfway_point)
    value_grad_blk = (
        token_wise(rate_blk) * mixed_dot("nhts,nthv->nshv", group_inverse, value_rounding)
    ).astype(halfway_point)
    score_gradient = (mixed_dot("nthv,nshv->nhts", grad_blk, fresh_values) * decay_mask).astype(
        halfway_point
    )
    write_gradient = (-mixed_dot("nthv,nhkv->nthk", value_rounding, state_heads)).astype(
        halfway_point
    )
    state_rounding = state_gradient.astype(halfway_point)
    query_grad_blk = (
        token_wise(incoming_decay) * mixed_dot("nthv,nhkv->nthk", grad_blk, state_heads)
        + mixed_dot("nhts,nshk->nthk", score_gradient, key_blk)
    ).astype(halfway_point)
    key_grad_blk = (
        mixed_dot("nhts,nthk->nshk", score_gradient, query_blk)
        + token_wise(outgoing_decay) * mixed_dot("nthv,nhkv->nthk", fresh_values, state_rounding)
        + token_wise(rate_blk * incoming_decay)
        * mixed_dot("nhts,nthk->nshk", group_inverse, write_gradient)
    ).astype(halfway_point)
    query_grad_heads = query_grad_blk.reshape(token_count, head_local, key_width)
    key_grad_heads = key_grad_blk.reshape(token_count, head_local, key_width)
    grad_value = value_grad_blk.reshape(token_count, head_local, value_width)
    grad_query, grad_key = (
        lax.all_to_all(query_grad_heads, "key", split_axis=2, concat_axis=1, tiled=True),
        lax.all_to_all(key_grad_heads, "key", split_axis=2, concat_axis=1, tiled=True),
    )
    value_square = square_sum(grad_value)
    partial_value = square_sum(grad_query) + square_sum(grad_key) + value_square
    summed = lax.psum(partial_value, ("seq", "key"))
    entries = (
        token_count * lax.axis_size("seq") * query_rows.shape[1] * (2 * key_width + value_width)
    )
    return (grad_query, grad_key, grad_value, summed / entries)


def solution(mesh):
    in_specs = (
        P("seq", None, "key"),
        P("seq", None, "key"),
        P("seq", "key", None),
        P("seq", "key", None),
        P("key", "seq"),
        P("key", "seq"),
        P("seq", "key", None, None),
        P("seq", None, "key", None),
    )
    out_specs = (P("seq", None, "key"), P("seq", None, "key"), P("seq", "key", None), P())
    return jax.shard_map(local, mesh=mesh, in_specs=in_specs, out_specs=out_specs, check_vma=False)
```

profile of v0, /device:TPU:1, one launch (start us, length us, event | category | flops | bytes accessed | tf_op | source)
XLA Modules:
  0.0 631.2 jit_solution(10819537718962490288)
XLA Ops:
  0.7 15.9 %all-to-all-start.1 = ((bf16[256,16,16]{0,2,1:T(8,128)(2,1)}), bf16[256,16,16]{0,2,1:T(8,128)(2,1)S(1)}, u32[]{:S(2)}, u32[]{:S(2)}) async-start(bf16[256,16,16]{0,2,1:T(8,128)(2,1)} %param.15), calls=%async_computation.1 | async-start | bytes 262144 | tf_op jit(solution)/shard_map/all_to_all | solution.py:53
  17.9 10.7 %all-to-all-done.1 = bf16[256,16,16]{0,2,1:T(8,128)(2,1)S(1)} async-done(((bf16[256,16,16]{0,2,1:T(8,128)(2,1)}), bf16[256,16,16]{0,2,1:T(8,128)(2,1)S(1)}, u32[]{:S(2)}, u32[]{:S(2)}) %all-to-all-start.1) | async-done | bytes 131104 | tf_op jit(solution)/shard_map/all_to_all | solution.py:53
  36.8 9.7 %all-to-all-done.3 = bf16[256,16,16]{0,2,1:T(8,128)(2,1)S(1)} async-done(((bf16[256,16,16]{0,2,1:T(8,128)(2,1)}), bf16[256,16,16]{0,2,1:T(8,128)(2,1)S(1)}, u32[]{:S(2)}, u32[]{:S(2)}) %all-to-all-start.3) | async-done | bytes 131104 | tf_op jit(solution)/shard_map/all_to_all | solution.py:52
  54.0 393.7 %while.57 = (s32[]{:T(128)}, f32[1,256,256]{2,1,0:T(8,128)S(1)}, f32[2,1]{0,1:T(1,128)S(1)}, bf16[2,128,1,256]{3,1,2,0:T(8,128)(2,1)S(1)}, bf16[2,128,1,256]{3,1...) while((s32[]{:T(128)}, f32[1,256,256]{2,1,0:T(8,128)S(1)}, ...), condition=%wide.region_4.5_spmd, body=%wide.region_1.4_spmd.sunk | while | flops 201523200 | bytes 3015986 | solution.py:97
  222.6 7.9 %collective-permute-done = f32[1,256,256]{2,1,0:T(8,128)S(1)} collective-permute-done((f32[1,256,256]{2,1,0:T(8,128)S(1)}, f32[1,256,256]{2,1,0:T(8,128)S(1)}, u32[]{:S(2)}, u32[]{:S(2)}) %collective-permute-start) | collective-permute-done | bytes 262176 | tf_op jit(solution)/shard_map/while/body/eval_jaxpr/ppermute | solution.py:12
  236.2 7.9 %collective-permute-done = f32[1,256,256]{2,1,0:T(8,128)S(1)} collective-permute-done((f32[1,256,256]{2,1,0:T(8,128)S(1)}, f32[1,256,256]{2,1,0:T(8,128)S(1)}, u32[]{:S(2)}, u32[]{:S(2)}) %collective-permute-start) | collective-permute-done | bytes 262176 | tf_op jit(solution)/shard_map/while/body/eval_jaxpr/ppermute | solution.py:12
  249.8 7.9 %collective-permute-done = f32[1,256,256]{2,1,0:T(8,128)S(1)} collective-permute-done((f32[1,256,256]{2,1,0:T(8,128)S(1)}, f32[1,256,256]{2,1,0:T(8,128)S(1)}, u32[]{:S(2)}, u32[]{:S(2)}) %collective-permute-start) | collective-permute-done | bytes 262176 | tf_op jit(solution)/shard_map/while/body/eval_jaxpr/ppermute | solution.py:12
  263.4 7.9 %collective-permute-done = f32[1,256,256]{2,1,0:T(8,128)S(1)} collective-permute-done((f32[1,256,256]{2,1,0:T(8,128)S(1)}, f32[1,256,256]{2,1,0:T(8,128)S(1)}, u32[]{:S(2)}, u32[]{:S(2)}) %collective-permute-start) | collective-permute-done | bytes 262176 | tf_op jit(solution)/shard_map/while/body/eval_jaxpr/ppermute | solution.py:12
  276.9 7.9 %collective-permute-done = f32[1,256,256]{2,1,0:T(8,128)S(1)} collective-permute-done((f32[1,256,256]{2,1,0:T(8,128)S(1)}, f32[1,256,256]{2,1,0:T(8,128)S(1)}, u32[]{:S(2)}, u32[]{:S(2)}) %collective-permute-start) | collective-permute-done | bytes 262176 | tf_op jit(solution)/shard_map/while/body/eval_jaxpr/ppermute | solution.py:12
  290.5 7.9 %collective-permute-done = f32[1,256,256]{2,1,0:T(8,128)S(1)} collective-permute-done((f32[1,256,256]{2,1,0:T(8,128)S(1)}, f32[1,256,256]{2,1,0:T(8,128)S(1)}, u32[]{:S(2)}, u32[]{:S(2)}) %collective-permute-start) | collective-permute-done | bytes 262176 | tf_op jit(solution)/shard_map/while/body/eval_jaxpr/ppermute | solution.py:12
  304.1 7.9 %collective-permute-done = f32[1,256,256]{2,1,0:T(8,128)S(1)} collective-permute-done((f32[1,256,256]{2,1,0:T(8,128)S(1)}, f32[1,256,256]{2,1,0:T(8,128)S(1)}, u32[]{:S(2)}, u32[]{:S(2)}) %collective-permute-start) | collective-permute-done | bytes 262176 | tf_op jit(solution)/shard_map/while/body/eval_jaxpr/ppermute | solution.py:12
  317.7 7.9 %collective-permute-done = f32[1,256,256]{2,1,0:T(8,128)S(1)} collective-permute-done((f32[1,256,256]{2,1,0:T(8,128)S(1)}, f32[1,256,256]{2,1,0:T(8,128)S(1)}, u32[]{:S(2)}, u32[]{:S(2)}) %collective-permute-start) | collective-permute-done | bytes 262176 | tf_op jit(solution)/shard_map/while/body/eval_jaxpr/ppermute | solution.py:12
  331.2 7.9 %collective-permute-done = f32[1,256,256]{2,1,0:T(8,128)S(1)} collective-permute-done((f32[1,256,256]{2,1,0:T(8,128)S(1)}, f32[1,256,256]{2,1,0:T(8,128)S(1)}, u32[]{:S(2)}, u32[]{:S(2)}) %collective-permute-start) | collective-permute-done | bytes 262176 | tf_op jit(solution)/shard_map/while/body/eval_jaxpr/ppermute | solution.py:12
  344.8 7.9 %collective-permute-done = f32[1,256,256]{2,1,0:T(8,128)S(1)} collective-permute-done((f32[1,256,256]{2,1,0:T(8,128)S(1)}, f32[1,256,256]{2,1,0:T(8,128)S(1)}, u32[]{:S(2)}, u32[]{:S(2)}) %collective-permute-start) | collective-permute-done | bytes 262176 | tf_op jit(solution)/shard_map/while/body/eval_jaxpr/ppermute | solution.py:12
  358.4 7.9 %collective-permute-done = f32[1,256,256]{2,1,0:T(8,128)S(1)} collective-permute-done((f32[1,256,256]{2,1,0:T(8,128)S(1)}, f32[1,256,256]{2,1,0:T(8,128)S(1)}, u32[]{:S(2)}, u32[]{:S(2)}) %collective-permute-start) | collective-permute-done | bytes 262176 | tf_op jit(solution)/shard_map/while/body/eval_jaxpr/ppermute | solution.py:12
  372.0 7.9 %collective-permute-done = f32[1,256,256]{2,1,0:T(8,128)S(1)} collective-permute-done((f32[1,256,256]{2,1,0:T(8,128)S(1)}, f32[1,256,256]{2,1,0:T(8,128)S(1)}, u32[]{:S(2)}, u32[]{:S(2)}) %collective-permute-start) | collective-permute-done | bytes 262176 | tf_op jit(solution)/shard_map/while/body/eval_jaxpr/ppermute | solution.py:12
  385.5 7.9 %collective-permute-done = f32[1,256,256]{2,1,0:T(8,128)S(1)} collective-permute-done((f32[1,256,256]{2,1,0:T(8,128)S(1)}, f32[1,256,256]{2,1,0:T(8,128)S(1)}, u32[]{:S(2)}, u32[]{:S(2)}) %collective-permute-start) | collective-permute-done | bytes 262176 | tf_op jit(solution)/shard_map/while/body/eval_jaxpr/ppermute | solution.py:12
  412.7 7.9 %collective-permute-done = f32[1,256,256]{2,1,0:T(8,128)S(1)} collective-permute-done((f32[1,256,256]{2,1,0:T(8,128)S(1)}, f32[1,256,256]{2,1,0:T(8,128)S(1)}, u32[]{:S(2)}, u32[]{:S(2)}) %collective-permute-start) | collective-permute-done | bytes 262176 | tf_op jit(solution)/shard_map/while/body/eval_jaxpr/ppermute | solution.py:12
  426.2 7.9 %collective-permute-done = f32[1,256,256]{2,1,0:T(8,128)S(1)} collective-permute-done((f32[1,256,256]{2,1,0:T(8,128)S(1)}, f32[1,256,256]{2,1,0:T(8,128)S(1)}, u32[]{:S(2)}, u32[]{:S(2)}) %collective-permute-start) | collective-permute-done | bytes 262176 | tf_op jit(solution)/shard_map/while/body/eval_jaxpr/ppermute | solution.py:12
  439.8 7.9 %collective-permute-done = f32[1,256,256]{2,1,0:T(8,128)S(1)} collective-permute-done((f32[1,256,256]{2,1,0:T(8,128)S(1)}, f32[1,256,256]{2,1,0:T(8,128)S(1)}, u32[]{:S(2)}, u32[]{:S(2)}) %collective-permute-start) | collective-permute-done | bytes 262176 | tf_op jit(solution)/shard_map/while/body/eval_jaxpr/ppermute | solution.py:12
  456.1 11.2 %all-to-all-start.4 = ((bf16[16,2,2048]{2,1,0:T(2,128)(2,1)}), bf16[16,2,2048]{2,1,0:T(2,128)(2,1)S(1)}, u32[]{:S(2)}, u32[]{:S(2)}) async-start(bf16[16,2,2048]{2,1,0:T(2,128)(2,1)} %reshape.369), calls=%async_computation.4 | async-start | bytes 262144 | tf_op jit(solution)/shard_map/all_to_all | solution.py:127
  470.0 9.2 %all-to-all-done.4 = bf16[16,2,2048]{2,1,0:T(2,128)(2,1)S(1)} async-done(((bf16[16,2,2048]{2,1,0:T(2,128)(2,1)}), bf16[16,2,2048]{2,1,0:T(2,128)(2,1)S(1)}, u32[]{:S(2)}, u32[]{:S(2)}) %all-to-all-start.4) | async-done | bytes 131104 | tf_op jit(solution)/shard_map/all_to_all | solution.py:127
  484.6 10.4 %all-to-all-done.2 = bf16[16,2,2048]{2,1,0:T(2,128)(2,1)S(1)} async-done(((bf16[16,2,2048]{2,1,0:T(2,128)(2,1)}), bf16[16,2,2048]{2,1,0:T(2,128)(2,1)S(1)}, u32[]{:S(2)}, u32[]{:S(2)}) %all-to-all-start.2) | async-done | bytes 131104 | tf_op jit(solution)/shard_map/all_to_all | solution.py:126
  498.3 129.8 %psum.7 = f32[]{:T(128)} all-reduce(f32[]{:T(128)S(6)} %add.89), channel_id=1, replica_groups=mesh['seq'=32,'key'=16] {'seq','key'}, use_global_device_ids=true, to_apply=%region_10.11 | all-reduce | flops 1 | bytes 8 | tf_op jit(solution)/shard_map/psum | solution.py:131
  (363 shorter events, 420.2 us)
Async XLA Ops:
  0.7 27.9 %all-to-all-start.1 = ((bf16[256,16,16]{0,2,1:T(8,128)(2,1)}), bf16[256,16,16]{0,2,1:T(8,128)(2,1)S(1)}, u32[]{:S(2)}, u32[]{:S(2)}) async-start(bf16[256,16,16]{0,2,1:T(8,128)(2,1)} %param.15), calls=%async_computation.1 | async-start | bytes 262144 | tf_op jit(solution)/shard_map/all_to_all | solution.py:53
  28.6 17.9 %all-to-all-start.3 = ((bf16[256,16,16]{0,2,1:T(8,128)(2,1)}), bf16[256,16,16]{0,2,1:T(8,128)(2,1)S(1)}, u32[]{:S(2)}, u32[]{:S(2)}) async-start(bf16[256,16,16]{0,2,1:T(8,128)(2,1)} %param.14), calls=%async_computation.3 | async-start | bytes 262144 | tf_op jit(solution)/shard_map/all_to_all | solution.py:52
  46.5 405.4 %all-to-all-start = ((bf16[2,16,16,256]{3,2,0,1:T(8,128)(2,1)}), bf16[2,16,16,256]{3,2,0,1:T(8,128)(2,1)S(1)}, u32[]{:S(2)}, u32[]{:S(2)}) async-start(bf16[2,16,16,256]{3,2,0,1:T(8,128)(2,1)} %copy.117), calls=%async_computation | async-start | bytes 524288 | tf_op jit(solution)/shard_map/all_to_all | solution.py:54
  57.7 9.4 %collective-permute-start = (f32[1,256,256]{2,1,0:T(8,128)S(1)}, f32[1,256,256]{2,1,0:T(8,128)S(1)}, u32[]{:S(2)}, u32[]{:S(2)}) collective-permute-start(f32[1,256,256]{2,1,0:T(8,128)S(1)} %get-tuple-element.637), channel_id=1, source_target_pairs={{16,0},{32,16},{48,32},{64,48},{80,64},{96,80},{112,96},{128,112},... | collective-permute-start | bytes 786440 | tf_op jit(solution)/shard_map/while/body/eval_jaxpr/ppermute | solution.py:12
  208.5 8.4 %collective-permute-start = (f32[1,256,256]{2,1,0:T(8,128)S(1)}, f32[1,256,256]{2,1,0:T(8,128)S(1)}, u32[]{:S(2)}, u32[]{:S(2)}) collective-permute-start(f32[1,256,256]{2,1,0:T(8,128)S(1)} %get-tuple-element.637), channel_id=1, source_target_pairs={{16,0},{32,16},{48,32},{64,48},{80,64},{96,80},{112,96},{128,112},... | collective-permute-start | bytes 786440 | tf_op jit(solution)/shard_map/while/body/eval_jaxpr/ppermute | solution.py:12
  220.7 9.8 %collective-permute-start = (f32[1,256,256]{2,1,0:T(8,128)S(1)}, f32[1,256,256]{2,1,0:T(8,128)S(1)}, u32[]{:S(2)}, u32[]{:S(2)}) collective-permute-start(f32[1,256,256]{2,1,0:T(8,128)S(1)} %get-tuple-element.637), channel_id=1, source_target_pairs={{16,0},{32,16},{48,32},{64,48},{80,64},{96,80},{112,96},{128,112},... | collective-permute-start | bytes 786440 | tf_op jit(solution)/shard_map/while/body/eval_jaxpr/ppermute | solution.py:12
  234.3 9.8 %collective-permute-start = (f32[1,256,256]{2,1,0:T(8,128)S(1)}, f32[1,256,256]{2,1,0:T(8,128)S(1)}, u32[]{:S(2)}, u32[]{:S(2)}) collective-permute-start(f32[1,256,256]{2,1,0:T(8,128)S(1)} %get-tuple-element.637), channel_id=1, source_target_pairs={{16,0},{32,16},{48,32},{64,48},{80,64},{96,80},{112,96},{128,112},... | collective-permute-start | bytes 786440 | tf_op jit(solution)/shard_map/while/body/eval_jaxpr/ppermute | solution.py:12
  247.9 9.8 %collective-permute-start = (f32[1,256,256]{2,1,0:T(8,128)S(1)}, f32[1,256,256]{2,1,0:T(8,128)S(1)}, u32[]{:S(2)}, u32[]{:S(2)}) collective-permute-start(f32[1,256,256]{2,1,0:T(8,128)S(1)} %get-tuple-element.637), channel_id=1, source_target_pairs={{16,0},{32,16},{48,32},{64,48},{80,64},{96,80},{112,96},{128,112},... | collective-permute-start | bytes 786440 | tf_op jit(solution)/shard_map/while/body/eval_jaxpr/ppermute | solution.py:12
  261.4 9.8 %collective-permute-start = (f32[1,256,256]{2,1,0:T(8,128)S(1)}, f32[1,256,256]{2,1,0:T(8,128)S(1)}, u32[]{:S(2)}, u32[]{:S(2)}) collective-permute-start(f32[1,256,256]{2,1,0:T(8,128)S(1)} %get-tuple-element.637), channel_id=1, source_target_pairs={{16,0},{32,16},{48,32},{64,48},{80,64},{96,80},{112,96},{128,112},... | collective-permute-start | bytes 786440 | tf_op jit(solution)/shard_map/while/body/eval_jaxpr/ppermute | solution.py:12
  275.0 9.8 %collective-permute-start = (f32[1,256,256]{2,1,0:T(8,128)S(1)}, f32[1,256,256]{2,1,0:T(8,128)S(1)}, u32[]{:S(2)}, u32[]{:S(2)}) collective-permute-start(f32[1,256,256]{2,1,0:T(8,128)S(1)} %get-tuple-element.637), channel_id=1, source_target_pairs={{16,0},{32,16},{48,32},{64,48},{80,64},{96,80},{112,96},{128,112},... | collective-permute-start | bytes 786440 | tf_op jit(solution)/shard_map/while/body/eval_jaxpr/ppermute | solution.py:12
  288.6 9.8 %collective-permute-start = (f32[1,256,256]{2,1,0:T(8,128)S(1)}, f32[1,256,256]{2,1,0:T(8,128)S(1)}, u32[]{:S(2)}, u32[]{:S(2)}) collective-permute-start(f32[1,256,256]{2,1,0:T(8,128)S(1)} %get-tuple-element.637), channel_id=1, source_target_pairs={{16,0},{32,16},{48,32},{64,48},{80,64},{96,80},{112,96},{128,112},... | collective-permute-start | bytes 786440 | tf_op jit(solution)/shard_map/while/body/eval_jaxpr/ppermute | solution.py:12
  302.2 9.8 %collective-permute-start = (f32[1,256,256]{2,1,0:T(8,128)S(1)}, f32[1,256,256]{2,1,0:T(8,128)S(1)}, u32[]{:S(2)}, u32[]{:S(2)}) collective-permute-start(f32[1,256,256]{2,1,0:T(8,128)S(1)} %get-tuple-element.637), channel_id=1, source_target_pairs={{16,0},{32,16},{48,32},{64,48},{80,64},{96,80},{112,96},{128,112},... | collective-permute-start | bytes 786440 | tf_op jit(solution)/shard_map/while/body/eval_jaxpr/ppermute | solution.py:12
  315.7 9.8 %collective-permute-start = (f32[1,256,256]{2,1,0:T(8,128)S(1)}, f32[1,256,256]{2,1,0:T(8,128)S(1)}, u32[]{:S(2)}, u32[]{:S(2)}) collective-permute-start(f32[1,256,256]{2,1,0:T(8,128)S(1)} %get-tuple-element.637), channel_id=1, source_target_pairs={{16,0},{32,16},{48,32},{64,48},{80,64},{96,80},{112,96},{128,112},... | collective-permute-start | bytes 786440 | tf_op jit(solution)/shard_map/while/body/eval_jaxpr/ppermute | solution.py:12
  329.3 9.8 %collective-permute-start = (f32[1,256,256]{2,1,0:T(8,128)S(1)}, f32[1,256,256]{2,1,0:T(8,128)S(1)}, u32[]{:S(2)}, u32[]{:S(2)}) collective-permute-start(f32[1,256,256]{2,1,0:T(8,128)S(1)} %get-tuple-element.637), channel_id=1, source_target_pairs={{16,0},{32,16},{48,32},{64,48},{80,64},{96,80},{112,96},{128,112},... | collective-permute-start | bytes 786440 | tf_op jit(solution)/shard_map/while/body/eval_jaxpr/ppermute | solution.py:12
  342.9 9.8 %collective-permute-start = (f32[1,256,256]{2,1,0:T(8,128)S(1)}, f32[1,256,256]{2,1,0:T(8,128)S(1)}, u32[]{:S(2)}, u32[]{:S(2)}) collective-permute-start(f32[1,256,256]{2,1,0:T(8,128)S(1)} %get-tuple-element.637), channel_id=1, source_target_pairs={{16,0},{32,16},{48,32},{64,48},{80,64},{96,80},{112,96},{128,112},... | collective-permute-start | bytes 786440 | tf_op jit(solution)/shard_map/while/body/eval_jaxpr/ppermute | solution.py:12
  356.5 9.8 %collective-permute-start = (f32[1,256,256]{2,1,0:T(8,128)S(1)}, f32[1,256,256]{2,1,0:T(8,128)S(1)}, u32[]{:S(2)}, u32[]{:S(2)}) collective-permute-start(f32[1,256,256]{2,1,0:T(8,128)S(1)} %get-tuple-element.637), channel_id=1, source_target_pairs={{16,0},{32,16},{48,32},{64,48},{80,64},{96,80},{112,96},{128,112},... | collective-permute-start | bytes 786440 | tf_op jit(solution)/shard_map/while/body/eval_jaxpr/ppermute | solution.py:12
  370.0 9.8 %collective-permute-start = (f32[1,256,256]{2,1,0:T(8,128)S(1)}, f32[1,256,256]{2,1,0:T(8,128)S(1)}, u32[]{:S(2)}, u32[]{:S(2)}) collective-permute-start(f32[1,256,256]{2,1,0:T(8,128)S(1)} %get-tuple-element.637), channel_id=1, source_target_pairs={{16,0},{32,16},{48,32},{64,48},{80,64},{96,80},{112,96},{128,112},... | collective-permute-start | bytes 786440 | tf_op jit(solution)/shard_map/while/body/eval_jaxpr/ppermute | solution.py:12
  383.6 9.8 %collective-permute-start = (f32[1,256,256]{2,1,0:T(8,128)S(1)}, f32[1,256,256]{2,1,0:T(8,128)S(1)}, u32[]{:S(2)}, u32[]{:S(2)}) collective-permute-start(f32[1,256,256]{2,1,0:T(8,128)S(1)} %get-tuple-element.637), channel_id=1, source_target_pairs={{16,0},{32,16},{48,32},{64,48},{80,64},{96,80},{112,96},{128,112},... | collective-permute-start | bytes 786440 | tf_op jit(solution)/shard_map/while/body/eval_jaxpr/ppermute | solution.py:12
  397.2 9.8 %collective-permute-start = (f32[1,256,256]{2,1,0:T(8,128)S(1)}, f32[1,256,256]{2,1,0:T(8,128)S(1)}, u32[]{:S(2)}, u32[]{:S(2)}) collective-permute-start(f32[1,256,256]{2,1,0:T(8,128)S(1)} %get-tuple-element.637), channel_id=1, source_target_pairs={{16,0},{32,16},{48,32},{64,48},{80,64},{96,80},{112,96},{128,112},... | collective-permute-start | bytes 786440 | tf_op jit(solution)/shard_map/while/body/eval_jaxpr/ppermute | solution.py:12
  410.7 9.8 %collective-permute-start = (f32[1,256,256]{2,1,0:T(8,128)S(1)}, f32[1,256,256]{2,1,0:T(8,128)S(1)}, u32[]{:S(2)}, u32[]{:S(2)}) collective-permute-start(f32[1,256,256]{2,1,0:T(8,128)S(1)} %get-tuple-element.637), channel_id=1, source_target_pairs={{16,0},{32,16},{48,32},{64,48},{80,64},{96,80},{112,96},{128,112},... | collective-permute-start | bytes 786440 | tf_op jit(solution)/shard_map/while/body/eval_jaxpr/ppermute | solution.py:12
  424.3 9.8 %collective-permute-start = (f32[1,256,256]{2,1,0:T(8,128)S(1)}, f32[1,256,256]{2,1,0:T(8,128)S(1)}, u32[]{:S(2)}, u32[]{:S(2)}) collective-permute-start(f32[1,256,256]{2,1,0:T(8,128)S(1)} %get-tuple-element.637), channel_id=1, source_target_pairs={{16,0},{32,16},{48,32},{64,48},{80,64},{96,80},{112,96},{128,112},... | collective-permute-start | bytes 786440 | tf_op jit(solution)/shard_map/while/body/eval_jaxpr/ppermute | solution.py:12
  437.9 9.8 %collective-permute-start = (f32[1,256,256]{2,1,0:T(8,128)S(1)}, f32[1,256,256]{2,1,0:T(8,128)S(1)}, u32[]{:S(2)}, u32[]{:S(2)}) collective-permute-start(f32[1,256,256]{2,1,0:T(8,128)S(1)} %get-tuple-element.637), channel_id=1, source_target_pairs={{16,0},{32,16},{48,32},{64,48},{80,64},{96,80},{112,96},{128,112},... | collective-permute-start | bytes 786440 | tf_op jit(solution)/shard_map/while/body/eval_jaxpr/ppermute | solution.py:12
  456.1 23.1 %all-to-all-start.4 = ((bf16[16,2,2048]{2,1,0:T(2,128)(2,1)}), bf16[16,2,2048]{2,1,0:T(2,128)(2,1)S(1)}, u32[]{:S(2)}, u32[]{:S(2)}) async-start(bf16[16,2,2048]{2,1,0:T(2,128)(2,1)} %reshape.369), calls=%async_computation.4 | async-start | bytes 262144 | tf_op jit(solution)/shard_map/all_to_all | solution.py:127
  479.2 15.8 %all-to-all-start.2 = ((bf16[16,2,2048]{2,1,0:T(2,128)(2,1)}), bf16[16,2,2048]{2,1,0:T(2,128)(2,1)S(1)}, u32[]{:S(2)}, u32[]{:S(2)}) async-start(bf16[16,2,2048]{2,1,0:T(2,128)(2,1)} %reshape.367), calls=%async_computation.2 | async-start | bytes 262144 | tf_op jit(solution)/shard_map/all_to_all | solution.py:126
  (18 other events, 181.4 us)
where the time goes:
time: 636 us; the launch traced here: 631 us
  waiting for transfers between devices  255 us (40%)
  blocking collectives  130 us (20%)
  starting transfers between devices  104 us (16%)
  matrix products  84.9 us (13%)
  local copies, waits for them, and re-layouts  45.3 us (7%)
    ppermute x31, waiting for transfers between devices, from_behind(): lax.ppermute(value, axis, [(source, source + steps) for source in range(f...  215 us
    psum x1, blocking collectives, local(): summed = lax.psum(partial_value, ('seq', 'key'))  130 us
    dot_general x130, matrix products, precise_product(): jnp.einsum(form, left.astype(jnp.float32), right, precision=highest_mode)  80.6 us
    ppermute x31, starting transfers between devices, from_behind(): lax.ppermute(value, axis, [(source, source + steps) for source in range(f...  61.5 us
    dynamic_slice x64, local copies, waits for them, and re-layouts, device_map(): lax.scan(group_step, state_out, (written_keys, key_result, end_decay, off...  37.6 us
    all_to_all x1, starting transfers between devices, local(): lax.all_to_all(key_rows, 'key', split_axis=1, concat_axis=2, tiled=True)  15.9 us
  transfers between devices with their start and end apart: 36, of which 35 were waited for; matrix products, arithmetic and copies ran while one was open for 20% of the time, Pallas kernels for 0%

commit v1 on v0

--- a/solution.py
+++ b/solution.py
@@ -128,7 +128,7 @@
     )
     value_square = square_sum(grad_value)
     partial_value = square_sum(grad_query) + square_sum(grad_key) + value_square
-    summed = lax.psum(partial_value, ("seq", "key"))
+    summed = lax.psum(lax.psum(partial_value, "key"), "seq")
     entries = (
         token_count * lax.axis_size("seq") * query_rows.shape[1] * (2 * key_width + value_width)
     )

time: 636 us -> 618 us (0.972)
  blocking collectives: 130 us -> 107 us
    psum x1 -> x2, blocking collectives: 130 us -> 107 us  [local(): summed = lax.psum(lax.psum(partial_value, 'key'), 'seq')]
  transfers between devices with their start and end apart: 36 -> 36, of which waited for: 35 -> 35; matrix products, arithmetic and copies ran while one was open for 20% -> 21% of each run, Pallas kernels for 0% -> 0%
where the time goes in v1:
time: 618 us; the launch traced here: 609 us
  waiting for transfers between devices  255 us (41%)
  blocking collectives  107 us (17%)
  starting transfers between devices  104 us (17%)
  matrix products  84.9 us (14%)
  local copies, waits for them, and re-layouts  45.3 us (7%)
    ppermute x31, waiting for transfers between devices, from_behind(): lax.ppermute(value, axis, [(source, source + steps) for source in range(f...  215 us
    psum x2, blocking collectives, local(): summed = lax.psum(lax.psum(partial_value, 'key'), 'seq')  107 us
    dot_general x130, matrix products, precise_product(): jnp.einsum(form, left.astype(jnp.float32), right, precision=highest_mode)  80.6 us
    ppermute x31, starting transfers between devices, from_behind(): lax.ppermute(value, axis, [(source, source + steps) for source in range(f...  61.5 us
    dynamic_slice x64, local copies, waits for them, and re-layouts, device_map(): lax.scan(group_step, state_out, (written_keys, key_result, end_decay, off...  37.6 us
    all_to_all x1, starting transfers between devices, local(): lax.all_to_all(key_rows, 'key', split_axis=1, concat_axis=2, tiled=True)  15.9 us
  transfers between devices with their start and end apart: 36, of which 35 were waited for; matrix products, arithmetic and copies ran while one was open for 21% of the time, Pallas kernels for 0%

profile of v1, /device:TPU:1, one launch (start us, length us, event | category | flops | bytes accessed | tf_op | source)
XLA Modules:
  0.0 608.8 jit_solution(8813328961810145554)
XLA Ops:
  0.7 15.9 %all-to-all-start.1 = ((bf16[256,16,16]{0,2,1:T(8,128)(2,1)}), bf16[256,16,16]{0,2,1:T(8,128)(2,1)S(1)}, u32[]{:S(2)}, u32[]{:S(2)}) async-start(bf16[256,16,16]{0,2,1:T(8,128)(2,1)} %param.15), calls=%async_computation.1 | async-start | bytes 262144 | tf_op jit(solution)/shard_map/all_to_all | solution.py:53
  17.9 10.7 %all-to-all-done.1 = bf16[256,16,16]{0,2,1:T(8,128)(2,1)S(1)} async-done(((bf16[256,16,16]{0,2,1:T(8,128)(2,1)}), bf16[256,16,16]{0,2,1:T(8,128)(2,1)S(1)}, u32[]{:S(2)}, u32[]{:S(2)}) %all-to-all-start.1) | async-done | bytes 131104 | tf_op jit(solution)/shard_map/all_to_all | solution.py:53
  36.8 9.7 %all-to-all-done.3 = bf16[256,16,16]{0,2,1:T(8,128)(2,1)S(1)} async-done(((bf16[256,16,16]{0,2,1:T(8,128)(2,1)}), bf16[256,16,16]{0,2,1:T(8,128)(2,1)S(1)}, u32[]{:S(2)}, u32[]{:S(2)}) %all-to-all-start.3) | async-done | bytes 131104 | tf_op jit(solution)/shard_map/all_to_all | solution.py:52
  54.0 393.7 %while.57 = (s32[]{:T(128)}, f32[1,256,256]{2,1,0:T(8,128)S(1)}, f32[2,1]{0,1:T(1,128)S(1)}, bf16[2,128,1,256]{3,1,2,0:T(8,128)(2,1)S(1)}, bf16[2,128,1,256]{3,1...) while((s32[]{:T(128)}, f32[1,256,256]{2,1,0:T(8,128)S(1)}, ...), condition=%wide.region_4.5_spmd, body=%wide.region_1.4_spmd.sunk | while | flops 201523200 | bytes 3015986 | solution.py:97
  222.6 7.9 %collective-permute-done = f32[1,256,256]{2,1,0:T(8,128)S(1)} collective-permute-done((f32[1,256,256]{2,1,0:T(8,128)S(1)}, f32[1,256,256]{2,1,0:T(8,128)S(1)}, u32[]{:S(2)}, u32[]{:S(2)}) %collective-permute-start) | collective-permute-done | bytes 262176 | tf_op jit(solution)/shard_map/while/body/eval_jaxpr/ppermute | solution.py:12
  236.2 7.9 %collective-permute-done = f32[1,256,256]{2,1,0:T(8,128)S(1)} collective-permute-done((f32[1,256,256]{2,1,0:T(8,128)S(1)}, f32[1,256,256]{2,1,0:T(8,128)S(1)}, u32[]{:S(2)}, u32[]{:S(2)}) %collective-permute-start) | collective-permute-done | bytes 262176 | tf_op jit(solution)/shard_map/while/body/eval_jaxpr/ppermute | solution.py:12
  249.8 7.9 %collective-permute-done = f32[1,256,256]{2,1,0:T(8,128)S(1)} collective-permute-done((f32[1,256,256]{2,1,0:T(8,128)S(1)}, f32[1,256,256]{2,1,0:T(8,128)S(1)}, u32[]{:S(2)}, u32[]{:S(2)}) %collective-permute-start) | collective-permute-done | bytes 262176 | tf_op jit(solution)/shard_map/while/body/eval_jaxpr/ppermute | solution.py:12
  263.4 7.9 %collective-permute-done = f32[1,256,256]{2,1,0:T(8,128)S(1)} collective-permute-done((f32[1,256,256]{2,1,0:T(8,128)S(1)}, f32[1,256,256]{2,1,0:T(8,128)S(1)}, u32[]{:S(2)}, u32[]{:S(2)}) %collective-permute-start) | collective-permute-done | bytes 262176 | tf_op jit(solution)/shard_map/while/body/eval_jaxpr/ppermute | solution.py:12
  276.9 7.9 %collective-permute-done = f32[1,256,256]{2,1,0:T(8,128)S(1)} collective-permute-done((f32[1,256,256]{2,1,0:T(8,128)S(1)}, f32[1,256,256]{2,1,0:T(8,128)S(1)}, u32[]{:S(2)}, u32[]{:S(2)}) %collective-permute-start) | collective-permute-done | bytes 262176 | tf_op jit(solution)/shard_map/while/body/eval_jaxpr/ppermute | solution.py:12
  290.5 7.9 %collective-permute-done = f32[1,256,256]{2,1,0:T(8,128)S(1)} collective-permute-done((f32[1,256,256]{2,1,0:T(8,128)S(1)}, f32[1,256,256]{2,1,0:T(8,128)S(1)}, u32[]{:S(2)}, u32[]{:S(2)}) %collective-permute-start) | collective-permute-done | bytes 262176 | tf_op jit(solution)/shard_map/while/body/eval_jaxpr/ppermute | solution.py:12
  304.1 7.9 %collective-permute-done = f32[1,256,256]{2,1,0:T(8,128)S(1)} collective-permute-done((f32[1,256,256]{2,1,0:T(8,128)S(1)}, f32[1,256,256]{2,1,0:T(8,128)S(1)}, u32[]{:S(2)}, u32[]{:S(2)}) %collective-permute-start) | collective-permute-done | bytes 262176 | tf_op jit(solution)/shard_map/while/body/eval_jaxpr/ppermute | solution.py:12
  317.7 7.9 %collective-permute-done = f32[1,256,256]{2,1,0:T(8,128)S(1)} collective-permute-done((f32[1,256,256]{2,1,0:T(8,128)S(1)}, f32[1,256,256]{2,1,0:T(8,128)S(1)}, u32[]{:S(2)}, u32[]{:S(2)}) %collective-permute-start) | collective-permute-done | bytes 262176 | tf_op jit(solution)/shard_map/while/body/eval_jaxpr/ppermute | solution.py:12
  331.2 7.9 %collective-permute-done = f32[1,256,256]{2,1,0:T(8,128)S(1)} collective-permute-done((f32[1,256,256]{2,1,0:T(8,128)S(1)}, f32[1,256,256]{2,1,0:T(8,128)S(1)}, u32[]{:S(2)}, u32[]{:S(2)}) %collective-permute-start) | collective-permute-done | bytes 262176 | tf_op jit(solution)/shard_map/while/body/eval_jaxpr/ppermute | solution.py:12
  344.8 7.9 %collective-permute-done = f32[1,256,256]{2,1,0:T(8,128)S(1)} collective-permute-done((f32[1,256,256]{2,1,0:T(8,128)S(1)}, f32[1,256,256]{2,1,0:T(8,128)S(1)}, u32[]{:S(2)}, u32[]{:S(2)}) %collective-permute-start) | collective-permute-done | bytes 262176 | tf_op jit(solution)/shard_map/while/body/eval_jaxpr/ppermute | solution.py:12
  358.4 7.9 %collective-permute-done = f32[1,256,256]{2,1,0:T(8,128)S(1)} collective-permute-done((f32[1,256,256]{2,1,0:T(8,128)S(1)}, f32[1,256,256]{2,1,0:T(8,128)S(1)}, u32[]{:S(2)}, u32[]{:S(2)}) %collective-permute-start) | collective-permute-done | bytes 262176 | tf_op jit(solution)/shard_map/while/body/eval_jaxpr/ppermute | solution.py:12
  385.5 7.9 %collective-permute-done = f32[1,256,256]{2,1,0:T(8,128)S(1)} collective-permute-done((f32[1,256,256]{2,1,0:T(8,128)S(1)}, f32[1,256,256]{2,1,0:T(8,128)S(1)}, u32[]{:S(2)}, u32[]{:S(2)}) %collective-permute-start) | collective-permute-done | bytes 262176 | tf_op jit(solution)/shard_map/while/body/eval_jaxpr/ppermute | solution.py:12
  399.1 7.9 %collective-permute-done = f32[1,256,256]{2,1,0:T(8,128)S(1)} collective-permute-done((f32[1,256,256]{2,1,0:T(8,128)S(1)}, f32[1,256,256]{2,1,0:T(8,128)S(1)}, u32[]{:S(2)}, u32[]{:S(2)}) %collective-permute-start) | collective-permute-done | bytes 262176 | tf_op jit(solution)/shard_map/while/body/eval_jaxpr/ppermute | solution.py:12
  412.7 7.9 %collective-permute-done = f32[1,256,256]{2,1,0:T(8,128)S(1)} collective-permute-done((f32[1,256,256]{2,1,0:T(8,128)S(1)}, f32[1,256,256]{2,1,0:T(8,128)S(1)}, u32[]{:S(2)}, u32[]{:S(2)}) %collective-permute-start) | collective-permute-done | bytes 262176 | tf_op jit(solution)/shard_map/while/body/eval_jaxpr/ppermute | solution.py:12
  439.8 7.9 %collective-permute-done = f32[1,256,256]{2,1,0:T(8,128)S(1)} collective-permute-done((f32[1,256,256]{2,1,0:T(8,128)S(1)}, f32[1,256,256]{2,1,0:T(8,128)S(1)}, u32[]{:S(2)}, u32[]{:S(2)}) %collective-permute-start) | collective-permute-done | bytes 262176 | tf_op jit(solution)/shard_map/while/body/eval_jaxpr/ppermute | solution.py:12
  456.1 11.2 %all-to-all-start.4 = ((bf16[16,2,2048]{2,1,0:T(2,128)(2,1)}), bf16[16,2,2048]{2,1,0:T(2,128)(2,1)S(1)}, u32[]{:S(2)}, u32[]{:S(2)}) async-start(bf16[16,2,2048]{2,1,0:T(2,128)(2,1)} %reshape.369), calls=%async_computation.4 | async-start | bytes 262144 | tf_op jit(solution)/shard_map/all_to_all | solution.py:127
  470.0 9.2 %all-to-all-done.4 = bf16[16,2,2048]{2,1,0:T(2,128)(2,1)S(1)} async-done(((bf16[16,2,2048]{2,1,0:T(2,128)(2,1)}), bf16[16,2,2048]{2,1,0:T(2,128)(2,1)S(1)}, u32[]{:S(2)}, u32[]{:S(2)}) %all-to-all-start.4) | async-done | bytes 131104 | tf_op jit(solution)/shard_map/all_to_all | solution.py:127
  484.6 10.4 %all-to-all-done.2 = bf16[16,2,2048]{2,1,0:T(2,128)(2,1)S(1)} async-done(((bf16[16,2,2048]{2,1,0:T(2,128)(2,1)}), bf16[16,2,2048]{2,1,0:T(2,128)(2,1)S(1)}, u32[]{:S(2)}, u32[]{:S(2)}) %all-to-all-start.2) | async-done | bytes 131104 | tf_op jit(solution)/shard_map/all_to_all | solution.py:126
  498.3 22.3 %psum.14 = f32[]{:T(128)} all-reduce(f32[]{:T(128)S(6)} %add.91), channel_id=1, replica_groups=mesh['seq'=32,'key'=16] {'key'}, use_global_device_ids=true, to_apply=%region_10.11 | all-reduce | flops 1 | bytes 8 | tf_op jit(solution)/shard_map/psum | solution.py:131
  520.5 85.1 %psum.15 = f32[]{:T(128)} all-reduce(f32[]{:T(128)} %psum.14), channel_id=1, replica_groups=mesh['seq'=32,'key'=16] {'seq'}, use_global_device_ids=true, to_apply=%region_11.12 | all-reduce | flops 1 | bytes 8 | tf_op jit(solution)/shard_map/psum | solution.py:131
  (364 shorter events, 428.1 us)
Async XLA Ops:
  0.7 27.9 %all-to-all-start.1 = ((bf16[256,16,16]{0,2,1:T(8,128)(2,1)}), bf16[256,16,16]{0,2,1:T(8,128)(2,1)S(1)}, u32[]{:S(2)}, u32[]{:S(2)}) async-start(bf16[256,16,16]{0,2,1:T(8,128)(2,1)} %param.15), calls=%async_computation.1 | async-start | bytes 262144 | tf_op jit(solution)/shard_map/all_to_all | solution.py:53
  28.6 17.9 %all-to-all-start.3 = ((bf16[256,16,16]{0,2,1:T(8,128)(2,1)}), bf16[256,16,16]{0,2,1:T(8,128)(2,1)S(1)}, u32[]{:S(2)}, u32[]{:S(2)}) async-start(bf16[256,16,16]{0,2,1:T(8,128)(2,1)} %param.14), calls=%async_computation.3 | async-start | bytes 262144 | tf_op jit(solution)/shard_map/all_to_all | solution.py:52
  46.5 405.4 %all-to-all-start = ((bf16[2,16,16,256]{3,2,0,1:T(8,128)(2,1)}), bf16[2,16,16,256]{3,2,0,1:T(8,128)(2,1)S(1)}, u32[]{:S(2)}, u32[]{:S(2)}) async-start(bf16[2,16,16,256]{3,2,0,1:T(8,128)(2,1)} %copy.117), calls=%async_computation | async-start | bytes 524288 | tf_op jit(solution)/shard_map/all_to_all | solution.py:54
  57.7 9.4 %collective-permute-start = (f32[1,256,256]{2,1,0:T(8,128)S(1)}, f32[1,256,256]{2,1,0:T(8,128)S(1)}, u32[]{:S(2)}, u32[]{:S(2)}) collective-permute-start(f32[1,256,256]{2,1,0:T(8,128)S(1)} %get-tuple-element.637), channel_id=1, source_target_pairs={{16,0},{32,16},{48,32},{64,48},{80,64},{96,80},{112,96},{128,112},... | collective-permute-start | bytes 786440 | tf_op jit(solution)/shard_map/while/body/eval_jaxpr/ppermute | solution.py:12
  208.5 8.4 %collective-permute-start = (f32[1,256,256]{2,1,0:T(8,128)S(1)}, f32[1,256,256]{2,1,0:T(8,128)S(1)}, u32[]{:S(2)}, u32[]{:S(2)}) collective-permute-start(f32[1,256,256]{2,1,0:T(8,128)S(1)} %get-tuple-element.637), channel_id=1, source_target_pairs={{16,0},{32,16},{48,32},{64,48},{80,64},{96,80},{112,96},{128,112},... | collective-permute-start | bytes 786440 | tf_op jit(solution)/shard_map/while/body/eval_jaxpr/ppermute | solution.py:12
  220.7 9.8 %collective-permute-start = (f32[1,256,256]{2,1,0:T(8,128)S(1)}, f32[1,256,256]{2,1,0:T(8,128)S(1)}, u32[]{:S(2)}, u32[]{:S(2)}) collective-permute-start(f32[1,256,256]{2,1,0:T(8,128)S(1)} %get-tuple-element.637), channel_id=1, source_target_pairs={{16,0},{32,16},{48,32},{64,48},{80,64},{96,80},{112,96},{128,112},... | collective-permute-start | bytes 786440 | tf_op jit(solution)/shard_map/while/body/eval_jaxpr/ppermute | solution.py:12
  234.3 9.8 %collective-permute-start = (f32[1,256,256]{2,1,0:T(8,128)S(1)}, f32[1,256,256]{2,1,0:T(8,128)S(1)}, u32[]{:S(2)}, u32[]{:S(2)}) collective-permute-start(f32[1,256,256]{2,1,0:T(8,128)S(1)} %get-tuple-element.637), channel_id=1, source_target_pairs={{16,0},{32,16},{48,32},{64,48},{80,64},{96,80},{112,96},{128,112},... | collective-permute-start | bytes 786440 | tf_op jit(solution)/shard_map/while/body/eval_jaxpr/ppermute | solution.py:12
  247.9 9.8 %collective-permute-start = (f32[1,256,256]{2,1,0:T(8,128)S(1)}, f32[1,256,256]{2,1,0:T(8,128)S(1)}, u32[]{:S(2)}, u32[]{:S(2)}) collective-permute-start(f32[1,256,256]{2,1,0:T(8,128)S(1)} %get-tuple-element.637), channel_id=1, source_target_pairs={{16,0},{32,16},{48,32},{64,48},{80,64},{96,80},{112,96},{128,112},... | collective-permute-start | bytes 786440 | tf_op jit(solution)/shard_map/while/body/eval_jaxpr/ppermute | solution.py:12
  261.4 9.8 %collective-permute-start = (f32[1,256,256]{2,1,0:T(8,128)S(1)}, f32[1,256,256]{2,1,0:T(8,128)S(1)}, u32[]{:S(2)}, u32[]{:S(2)}) collective-permute-start(f32[1,256,256]{2,1,0:T(8,128)S(1)} %get-tuple-element.637), channel_id=1, source_target_pairs={{16,0},{32,16},{48,32},{64,48},{80,64},{96,80},{112,96},{128,112},... | collective-permute-start | bytes 786440 | tf_op jit(solution)/shard_map/while/body/eval_jaxpr/ppermute | solution.py:12
  275.0 9.8 %collective-permute-start = (f32[1,256,256]{2,1,0:T(8,128)S(1)}, f32[1,256,256]{2,1,0:T(8,128)S(1)}, u32[]{:S(2)}, u32[]{:S(2)}) collective-permute-start(f32[1,256,256]{2,1,0:T(8,128)S(1)} %get-tuple-element.637), channel_id=1, source_target_pairs={{16,0},{32,16},{48,32},{64,48},{80,64},{96,80},{112,96},{128,112},... | collective-permute-start | bytes 786440 | tf_op jit(solution)/shard_map/while/body/eval_jaxpr/ppermute | solution.py:12
  288.6 9.8 %collective-permute-start = (f32[1,256,256]{2,1,0:T(8,128)S(1)}, f32[1,256,256]{2,1,0:T(8,128)S(1)}, u32[]{:S(2)}, u32[]{:S(2)}) collective-permute-start(f32[1,256,256]{2,1,0:T(8,128)S(1)} %get-tuple-element.637), channel_id=1, source_target_pairs={{16,0},{32,16},{48,32},{64,48},{80,64},{96,80},{112,96},{128,112},... | collective-permute-start | bytes 786440 | tf_op jit(solution)/shard_map/while/body/eval_jaxpr/ppermute | solution.py:12
  302.2 9.8 %collective-permute-start = (f32[1,256,256]{2,1,0:T(8,128)S(1)}, f32[1,256,256]{2,1,0:T(8,128)S(1)}, u32[]{:S(2)}, u32[]{:S(2)}) collective-permute-start(f32[1,256,256]{2,1,0:T(8,128)S(1)} %get-tuple-element.637), channel_id=1, source_target_pairs={{16,0},{32,16},{48,32},{64,48},{80,64},{96,80},{112,96},{128,112},... | collective-permute-start | bytes 786440 | tf_op jit(solution)/shard_map/while/body/eval_jaxpr/ppermute | solution.py:12
  315.7 9.8 %collective-permute-start = (f32[1,256,256]{2,1,0:T(8,128)S(1)}, f32[1,256,256]{2,1,0:T(8,128)S(1)}, u32[]{:S(2)}, u32[]{:S(2)}) collective-permute-start(f32[1,256,256]{2,1,0:T(8,128)S(1)} %get-tuple-element.637), channel_id=1, source_target_pairs={{16,0},{32,16},{48,32},{64,48},{80,64},{96,80},{112,96},{128,112},... | collective-permute-start | bytes 786440 | tf_op jit(solution)/shard_map/while/body/eval_jaxpr/ppermute | solution.py:12
  329.3 9.8 %collective-permute-start = (f32[1,256,256]{2,1,0:T(8,128)S(1)}, f32[1,256,256]{2,1,0:T(8,128)S(1)}, u32[]{:S(2)}, u32[]{:S(2)}) collective-permute-start(f32[1,256,256]{2,1,0:T(8,128)S(1)} %get-tuple-element.637), channel_id=1, source_target_pairs={{16,0},{32,16},{48,32},{64,48},{80,64},{96,80},{112,96},{128,112},... | collective-permute-start | bytes 786440 | tf_op jit(solution)/shard_map/while/body/eval_jaxpr/ppermute | solution.py:12
  342.9 9.8 %collective-permute-start = (f32[1,256,256]{2,1,0:T(8,128)S(1)}, f32[1,256,256]{2,1,0:T(8,128)S(1)}, u32[]{:S(2)}, u32[]{:S(2)}) collective-permute-start(f32[1,256,256]{2,1,0:T(8,128)S(1)} %get-tuple-element.637), channel_id=1, source_target_pairs={{16,0},{32,16},{48,32},{64,48},{80,64},{96,80},{112,96},{128,112},... | collective-permute-start | bytes 786440 | tf_op jit(solution)/shard_map/while/body/eval_jaxpr/ppermute | solution.py:12
  356.4 9.8 %collective-permute-start = (f32[1,256,256]{2,1,0:T(8,128)S(1)}, f32[1,256,256]{2,1,0:T(8,128)S(1)}, u32[]{:S(2)}, u32[]{:S(2)}) collective-permute-start(f32[1,256,256]{2,1,0:T(8,128)S(1)} %get-tuple-element.637), channel_id=1, source_target_pairs={{16,0},{32,16},{48,32},{64,48},{80,64},{96,80},{112,96},{128,112},... | collective-permute-start | bytes 786440 | tf_op jit(solution)/shard_map/while/body/eval_jaxpr/ppermute | solution.py:12
  370.0 9.8 %collective-permute-start = (f32[1,256,256]{2,1,0:T(8,128)S(1)}, f32[1,256,256]{2,1,0:T(8,128)S(1)}, u32[]{:S(2)}, u32[]{:S(2)}) collective-permute-start(f32[1,256,256]{2,1,0:T(8,128)S(1)} %get-tuple-element.637), channel_id=1, source_target_pairs={{16,0},{32,16},{48,32},{64,48},{80,64},{96,80},{112,96},{128,112},... | collective-permute-start | bytes 786440 | tf_op jit(solution)/shard_map/while/body/eval_jaxpr/ppermute | solution.py:12
  383.6 9.8 %collective-permute-start = (f32[1,256,256]{2,1,0:T(8,128)S(1)}, f32[1,256,256]{2,1,0:T(8,128)S(1)}, u32[]{:S(2)}, u32[]{:S(2)}) collective-permute-start(f32[1,256,256]{2,1,0:T(8,128)S(1)} %get-tuple-element.637), channel_id=1, source_target_pairs={{16,0},{32,16},{48,32},{64,48},{80,64},{96,80},{112,96},{128,112},... | collective-permute-start | bytes 786440 | tf_op jit(solution)/shard_map/while/body/eval_jaxpr/ppermute | solution.py:12
  397.2 9.8 %collective-permute-start = (f32[1,256,256]{2,1,0:T(8,128)S(1)}, f32[1,256,256]{2,1,0:T(8,128)S(1)}, u32[]{:S(2)}, u32[]{:S(2)}) collective-permute-start(f32[1,256,256]{2,1,0:T(8,128)S(1)} %get-tuple-element.637), channel_id=1, source_target_pairs={{16,0},{32,16},{48,32},{64,48},{80,64},{96,80},{112,96},{128,112},... | collective-permute-start | bytes 786440 | tf_op jit(solution)/shard_map/while/body/eval_jaxpr/ppermute | solution.py:12
  410.7 9.8 %collective-permute-start = (f32[1,256,256]{2,1,0:T(8,128)S(1)}, f32[1,256,256]{2,1,0:T(8,128)S(1)}, u32[]{:S(2)}, u32[]{:S(2)}) collective-permute-start(f32[1,256,256]{2,1,0:T(8,128)S(1)} %get-tuple-element.637), channel_id=1, source_target_pairs={{16,0},{32,16},{48,32},{64,48},{80,64},{96,80},{112,96},{128,112},... | collective-permute-start | bytes 786440 | tf_op jit(solution)/shard_map/while/body/eval_jaxpr/ppermute | solution.py:12
  424.3 9.8 %collective-permute-start = (f32[1,256,256]{2,1,0:T(8,128)S(1)}, f32[1,256,256]{2,1,0:T(8,128)S(1)}, u32[]{:S(2)}, u32[]{:S(2)}) collective-permute-start(f32[1,256,256]{2,1,0:T(8,128)S(1)} %get-tuple-element.637), channel_id=1, source_target_pairs={{16,0},{32,16},{48,32},{64,48},{80,64},{96,80},{112,96},{128,112},... | collective-permute-start | bytes 786440 | tf_op jit(solution)/shard_map/while/body/eval_jaxpr/ppermute | solution.py:12
  437.9 9.8 %collective-permute-start = (f32[1,256,256]{2,1,0:T(8,128)S(1)}, f32[1,256,256]{2,1,0:T(8,128)S(1)}, u32[]{:S(2)}, u32[]{:S(2)}) collective-permute-start(f32[1,256,256]{2,1,0:T(8,128)S(1)} %get-tuple-element.637), channel_id=1, source_target_pairs={{16,0},{32,16},{48,32},{64,48},{80,64},{96,80},{112,96},{128,112},... | collective-permute-start | bytes 786440 | tf_op jit(solution)/shard_map/while/body/eval_jaxpr/ppermute | solution.py:12
  456.1 23.1 %all-to-all-start.4 = ((bf16[16,2,2048]{2,1,0:T(2,128)(2,1)}), bf16[16,2,2048]{2,1,0:T(2,128)(2,1)S(1)}, u32[]{:S(2)}, u32[]{:S(2)}) async-start(bf16[16,2,2048]{2,1,0:T(2,128)(2,1)} %reshape.369), calls=%async_computation.4 | async-start | bytes 262144 | tf_op jit(solution)/shard_map/all_to_all | solution.py:127
  479.2 15.8 %all-to-all-start.2 = ((bf16[16,2,2048]{2,1,0:T(2,128)(2,1)}), bf16[16,2,2048]{2,1,0:T(2,128)(2,1)S(1)}, u32[]{:S(2)}, u32[]{:S(2)}) async-start(bf16[16,2,2048]{2,1,0:T(2,128)(2,1)} %reshape.367), calls=%async_computation.2 | async-start | bytes 262144 | tf_op jit(solution)/shard_map/all_to_all | solution.py:126
  (18 other events, 181.4 us)
